TPU v7x, 32 devices: a whole 2x2x4 slice. The times are simulated.
32 devices in a mesh: row: 4 (over y, core), col: 8 (over z, x).
Axes of the slice: x: 2, y: 2, z: 4, core: 2. Of those that a mesh axis runs over, the one named last changes fastest.
Arguments:
- child_fronts: float32 [20, 512, 20, 1024], P(None, 'col', None, 'row'), as said below
- parent_diagonal: float32 [16384], replicated, may hold values from 0.5 to 4
- block_maps: int32 [2, 20], replicated, may hold values from 0 to 31, as said below
Outputs:
- factored: float32 [16384, 16384], P('row', 'col')
Inputs may be any that keep to these rules, and one draw needn't show every extreme that they name: `child_fronts`: each child's matrix is symmetric and positive definite. `block_maps`: each row names 20 distinct front blocks in increasing order; every one of the 32 front blocks is named by at least one row, and exactly 8 of them by both rows.
All inputs are finite; a program needn't handle non-finite values.
Results may differ from a plain program's by a relative error of at most 0.0001.
Values sent between devices are 32-bit elements; how exact they have to be, the bound alone decides.
A program may use at most 320 MiB of HBM per device.

v0:
```python
import jax
import jax.numpy as jnp
from jax import lax
from jax.sharding import PartitionSpec as P

B = 512


def broadcast(x, axis, root):
    mine = lax.axis_index(axis) == root
    return lax.psum(jnp.where(mine, x, jnp.zeros_like(x)), axis)


def inverse_maps(block_maps, count):
    blocks = jnp.arange(count, dtype=jnp.int32)
    matches = block_maps[:, None, :] == blocks[None, :, None]
    present = jnp.any(matches, axis=2)
    places = jnp.arange(block_maps.shape[1], dtype=jnp.int32)
    source = jnp.sum(jnp.where(matches, places[None, None, :], 0), axis=2)
    return (source, present)


def shards(child_fronts, parent_diagonal, block_maps):
    row_count = lax.axis_size("row")
    column_count = lax.axis_size("col")
    row_index = lax.axis_index("row")
    column_index = lax.axis_index("col")
    half_count = row_count // 2
    blocks = parent_diagonal.shape[0] // B
    local_rows = blocks // row_count
    local_cols = blocks // column_count
    slice_rows = B // column_count
    slice_cols = 2 * B // row_count
    source, present = inverse_maps(block_maps, blocks)
    my_child = row_index // half_count
    my_source = lax.dynamic_index_in_dim(source, my_child, 0, keepdims=False)
    my_present = lax.dynamic_index_in_dim(present, my_child, 0, keepdims=False)
    picked_rows = jnp.take(child_fronts, my_source, axis=0)
    picked_both = jnp.take(picked_rows, my_source, axis=2)
    keep_mask = my_present[:, None, None, None] & my_present[None, None, :, None]
    picked_both = jnp.where(keep_mask, picked_both, 0.0)
    buffer = picked_both.reshape(
        local_rows, row_count, slice_rows, local_cols, column_count, slice_cols
    )
    buffer = buffer.transpose(1, 4, 0, 2, 3, 5).reshape(row_count * column_count, -1)
    received = lax.all_to_all(buffer, ("row", "col"), split_axis=0, concat_axis=0, tiled=True)
    received = received.reshape(
        2, half_count, column_count, local_rows, slice_rows, local_cols, slice_cols
    )
    summed = received[0] + received[1]
    frontal = summed.transpose(2, 1, 3, 4, 0, 5).reshape(local_rows, B, local_cols, B)
    row_blocks = jnp.arange(local_rows, dtype=jnp.int32) * row_count + row_index
    col_blocks = jnp.arange(local_cols, dtype=jnp.int32) * column_count + column_index
    diag_table = parent_diagonal.reshape(blocks, B)
    diag_rows = jnp.take(diag_table, row_blocks, axis=0)
    same_block = row_blocks[:, None] == col_blocks[None, :]
    identity = jnp.arange(B)[:, None] == jnp.arange(B)[None, :]
    diag_mask = same_block[:, None, :, None] & identity[None, :, None, :]
    frontal = frontal + jnp.where(diag_mask, diag_rows[:, :, None, None], 0.0)
    for panel_index in range(2):
        column_slab = frontal[:, :, panel_index // column_count, :]
        root_row = panel_index % row_count
        local_row = panel_index // row_count
        root_col = panel_index % column_count
        diagonal = broadcast(column_slab[local_row], "row", root_row)
        lower_factor = jnp.linalg.cholesky(diagonal)
        solved = jax.scipy.linalg.solve_triangular(
            lower_factor, column_slab.reshape(-1, B).T, lower=True
        ).T
        solved = solved.reshape(local_rows, B, B)
        factor_factor_column = jnp.where(
            (row_blocks > panel_index)[:, None, None],
            solved,
            jnp.where((row_blocks == panel_index)[:, None, None], lower_factor[None], 0.0),
        )
        factor_factor_column = broadcast(factor_factor_column, "col", root_col)
        owner_rows = (
            jnp.arange(local_cols, dtype=jnp.int32) * column_count + column_index
        ) // row_count
        factor_picked_rows = jnp.take(factor_factor_column, owner_rows, axis=0)
        factor_across = broadcast(factor_picked_rows, "row", column_index % row_count)
        section = frontal
        span_count = local_cols - 0
        product = lax.dot_general(
            factor_factor_column.reshape(-1, B),
            factor_across.reshape(-1, B),
            (((1,), (1,)), ((), ())),
            precision=lax.Precision.HIGHEST,
            preferred_element_type=jnp.float32,
        )
        product = product.reshape(local_rows, B, span_count, B)
        inside = (row_blocks > panel_index)[:, None, None, None] & (col_blocks > panel_index)[
            None, None, :, None
        ]
        section = jnp.where(inside, section - product, section)
        section = jnp.where(
            (col_blocks == panel_index)[None, None, :, None],
            factor_factor_column[:, :, None, :],
            section,
        )
        upper_mask = (row_blocks == panel_index)[:, None, None, None] & (col_blocks > panel_index)[
            None, None, :, None
        ]
        section = jnp.where(upper_mask, 0.0, section)
        frontal = frontal.at[:, :, 0:local_cols, :].set(section)
    return frontal.reshape(local_rows * B, local_cols * B)


def solution(mesh):
    return jax.shard_map(
        shards,
        mesh=mesh,
        in_specs=(P(None, "col", None, "row"), P(), P()),
        out_specs=P("row", "col"),
        check_vma=False,
    )
```

profile of v0, /device:TPU:0, one launch (start us, length us, event | category | flops | bytes accessed | tf_op | source)
XLA Modules:
  0.0 3438.4 jit_solution(6501763673328221221)
XLA Ops:
  7.6 28.1 gather_fusion
  35.7 29.5 broadcast_select_fusion
  65.2 43.3 %gather_fusion.1 = f32[32,32,64,256]{3,2,1,0:T(8,128)} fusion(f32[32,64,20,256]{3,1,2,0:T(8,128)} %broadcast_select_fusion, s32[1024]{0:T(1024)S(1)} %pad_clamp_fusion.2), kind=kCustom, calls=%fused_computation.3 | custom fusion | bytes 134217856 | tf_op jit(solution)/shard_map/jit(_take)/gather | solution.py:39
  109.2 74.0 %fusion.1 = f32[4,8,8,64,4,256]{5,4,3,2,1,0:T(4,128)} fusion(f32[8,4,64,4,8,256]{5,2,1,0,4,3:T(8,128)} %bitcast.4, pred[4,8]{0,1:T(8,128)(4,1)S(1)} %copy.55, pred[8,4,4,8]{2,0,3,1:T(8,128)(4,1)S(1)} %broadcast_and_fusion), kind=kLoop, calls=%fused_computation.11 | loop fusion | flops 33554432 | bytes 134218784 | tf_op jit(solution)/shard_map/transpose | solution.py:45
  183.2 83.9 %all_to_all.8 = f32[32,1,524288]{2,1,0:T(1,128)} reshape(f32[4,8,8,64,4,256]{5,4,3,2,1,0:T(4,128)} %fusion.1) | data formatting | bytes 134217728 | tf_op jit(solution)/shard_map/all_to_all | solution.py:46
  275.3 1444.8 %all-to-all-done = f32[32,1,524288]{2,1,0:T(1,128)} async-done(((f32[32,1,524288]{2,1,0:T(1,128)}), f32[32,1,524288]{2,1,0:T(1,128)}, u32[]{:S(2)}, u32[]{:S(2)}) %all-to-all-start) | async-done | bytes 67108896 | tf_op jit(solution)/shard_map/all_to_all | solution.py:46
  1720.1 110.6 %fusion.6 = f32[16,524288]{1,0:T(8,128)} fusion(f32[32,1,524288]{2,1,0:T(1,128)} %all-to-all-done), kind=kLoop, calls=%fused_computation.19 | loop fusion | flops 8388608 | bytes 100663296 | tf_op jit(solution)/shard_map/add | solution.py:50
  1830.7 59.3 %add.207 = f32[2,8,8,64,4,256]{5,4,3,2,1,0:T(4,128)} reshape(f32[16,524288]{1,0:T(8,128)} %fusion.6) | data formatting | bytes 67108864 | tf_op jit(solution)/shard_map/add | solution.py:50
  1890.1 44.6 %copy.78 = f32[8,8,64,4,2,256]{2,1,5,4,3,0:T(8,128)} copy(f32[8,8,64,4,2,256]{5,3,2,0,1,4:T(4,128)} %bitcast.149) | data formatting | bytes 67108864 | tf_op jit(solution)/shard_map/reshape | solution.py:51
  1934.7 54.5 %reshape.582 = f32[8,512,4,512]{1,3,2,0:T(8,128)} reshape(f32[8,8,64,4,2,256]{2,1,5,4,3,0:T(8,128)} %copy.78) | data formatting | bytes 67108864 | tf_op jit(solution)/shard_map/reshape | solution.py:51
  1989.2 14.0 select_add_fusion
  2003.3 11.7 copy-done
  2023.8 9.1 copy.61
  2032.9 9.1 copy.62
  2042.0 67.6 %all-reduce.8.cloned.1.call-done = f32[512,512]{0,1:T(8,128)} async-done(((f32[512,512]{0,1:T(8,128)}), f32[512,512]{0,1:T(8,128)}) %all-reduce.8.cloned.1.call-update) | async-done | bytes 1048592 | tf_op jit(solution)/shard_map/psum | solution.py:11
  2112.7 11.7 cholesky.286
  2124.5 9.8 custom-call.27
  2135.0 11.7 cholesky.305
  2146.8 10.2 custom-call.28
  2157.7 11.7 cholesky.326
  2170.0 9.8 custom-call.29
  2180.4 11.7 cholesky.343
  2204.0 39.3 %custom-call.30 = f32[4,128,128]{1,2,0:T(8,128)S(1)} custom-call(f32[4,128,128]{2,1,0:T(8,128)S(1)} %get-tuple-element.62), custom_call_target="InvertDiagBlocksLowerTriangular" | custom-call | tf_op jit(solution)/shard_map/jit(_solve_triangular)/triangular_solve | solution.py:67
  2269.6 9.0 copy.79
  2278.6 8.3 select_select_fusion.1
  2287.0 270.8 %all-reduce.10.cloned.1.call-done = f32[8,512,512]{2,1,0:T(8,128)} async-done(((f32[8,512,512]{2,1,0:T(8,128)}), f32[8,512,512]{2,1,0:T(8,128)}) %all-reduce.10.cloned.1.call-update) | async-done | bytes 8388624 | tf_op jit(solution)/shard_map/psum | solution.py:11
  2569.0 9.6 copy.64
  2578.6 74.9 %all-reduce.12.cloned.1.call-done = f32[4,512,512]{2,1,0:T(8,128)} async-done(((f32[4,512,512]{2,1,0:T(8,128)}), f32[4,512,512]{2,1,0:T(8,128)}) %all-reduce.12.cloned.1.call-update) | async-done | bytes 4194320 | tf_op jit(solution)/shard_map/psum | solution.py:11
  2653.5 62.6 %fusion.3 = f32[8,512,4,512]{1,3,2,0:T(8,128)} fusion(f32[8,512,4,512]{1,3,2,0:T(8,128)} %copy-done, f32[8,512,512]{1,2,0:T(8,128)} %copy.64, pred[4]{0:T(512)(128)(4,1)S(1)} %get-tuple-element.118, pred[8,4]{1,0:T(8,128)(4,1)S(1)} %get-tuple-element.111, pred[8,4]{1,0:T(8,128)(4,1)S(1)} %get-tuple-element.110, ...), kind=kOutput, calls=%fused_computation.15 | convolution fusion | flops 51573161984 | bytes 88080448 | tf_op jit(solution)/shard_map/dot_general | solution.py:84
  2726.2 9.2 copy.67
  2735.3 9.1 copy.68
  2744.5 10.4 all-reduce.14.cloned.1.call-done
  2758.0 11.7 cholesky.358
  2769.8 9.8 custom-call.31
  2780.3 11.7 cholesky.377
  2793.3 10.2 custom-call.32
  2804.2 11.7 cholesky.398
  2816.6 9.8 custom-call.33
  2827.0 11.7 cholesky.415
  2849.9 39.3 %custom-call.34 = f32[4,128,128]{1,2,0:T(8,128)S(1)} custom-call(f32[4,128,128]{2,1,0:T(8,128)S(1)} %get-tuple-element.63), custom_call_target="InvertDiagBlocksLowerTriangular" | custom-call | tf_op jit(solution)/shard_map/jit(_solve_triangular)/triangular_solve | solution.py:67
  2915.5 9.0 copy.69
  2924.5 8.3 select_select_fusion
  2932.8 270.9 %all-reduce.16.cloned.1.call-done = f32[8,512,512]{2,1,0:T(8,128)} async-done(((f32[8,512,512]{2,1,0:T(8,128)}), f32[8,512,512]{2,1,0:T(8,128)}) %all-reduce.16.cloned.1.call-update) | async-done | bytes 8388624 | tf_op jit(solution)/shard_map/psum | solution.py:11
  3214.9 9.2 copy.70
  3224.0 75.4 %all-reduce.18.cloned.1.call-done = f32[4,512,512]{2,1,0:T(8,128)} async-done(((f32[4,512,512]{2,1,0:T(8,128)}), f32[4,512,512]{2,1,0:T(8,128)}) %all-reduce.18.cloned.1.call-update) | async-done | bytes 4194320 | tf_op jit(solution)/shard_map/psum | solution.py:11
  3299.5 62.6 %fusion.5 = f32[8,512,4,512]{1,3,2,0:T(8,128)} fusion(f32[8,512,4,512]{1,3,2,0:T(8,128)} %fusion.3, f32[8,512,512]{1,2,0:T(8,128)} %copy.70, pred[4]{0:T(512)(128)(4,1)S(1)} %get-tuple-element.124, pred[8,4]{1,0:T(8,128)(4,1)S(1)} %get-tuple-element.109, pred[8,4]{1,0:T(8,128)(4,1)S(1)} %get-tuple-element.108, ...), kind=kOutput, calls=%fused_computation.17 | convolution fusion | flops 51573161984 | bytes 88080448 | tf_op jit(solution)/shard_map/dot_general | solution.py:84
  3362.1 39.0 %copy.80 = f32[8,512,4,512]{3,2,1,0:T(4,128)} copy(f32[8,512,4,512]{1,3,2,0:T(8,128)} %fusion.5) | data formatting | bytes 67108864 | tf_op jit(solution)/shard_map/reshape | solution.py:106
  3401.1 30.0 copy.85
  (146 shorter events, 149.6 us)
Async XLA Ops:
  267.1 7.3 copy-start.1
  267.1 1453.0 %all-to-all-start = ((f32[32,1,524288]{2,1,0:T(1,128)}), f32[32,1,524288]{2,1,0:T(1,128)}, u32[]{:S(2)}, u32[]{:S(2)}) async-start(f32[32,1,524288]{2,1,0:T(1,128)} %all_to_all.8), calls=%async_computation | async-start | bytes 134217728 | tf_op jit(solution)/shard_map/all_to_all | solution.py:46
  274.1 1835.5 %all-reduce.8.cloned.1.call-start = ((), (), s32[]{:S(2)}) async-start(), calls=%async_computation.1 | async-start | bytes 2097152 | tf_op jit(solution)/shard_map/psum | solution.py:11
  2003.3 11.7 copy-start
  2016.1 541.7 %all-reduce.10.cloned.1.call-start = ((), (), s32[]{:S(2)}) async-start(), calls=%async_computation.2 | async-start | bytes 16777216 | tf_op jit(solution)/shard_map/psum | solution.py:11
  2286.9 366.6 %all-reduce.12.cloned.1.call-start = ((), (), s32[]{:S(2)}) async-start(), calls=%async_computation.3 | async-start | bytes 8388608 | tf_op jit(solution)/shard_map/psum | solution.py:11
  2568.9 186.1 %all-reduce.14.cloned.1.call-start = ((), (), s32[]{:S(2)}) async-start(), calls=%async_computation.4 | async-start | bytes 2097152 | tf_op jit(solution)/shard_map/psum | solution.py:11
  2718.5 485.2 %all-reduce.16.cloned.1.call-start = ((), (), s32[]{:S(2)}) async-start(), calls=%async_computation.5 | async-start | bytes 16777216 | tf_op jit(solution)/shard_map/psum | solution.py:11
  2932.8 366.7 %all-reduce.18.cloned.1.call-start = ((), (), s32[]{:S(2)}) async-start(), calls=%async_computation.6 | async-start | bytes 8388608 | tf_op jit(solution)/shard_map/psum | solution.py:11
Sparse Core Ops, SparseCore 0:
  2016.2 93.3 all-reduce.7
  2287.0 270.7 all-reduce.9
  2569.0 84.5 all-reduce.11
  2718.6 36.2 all-reduce.13
  2932.9 270.7 all-reduce.15
  3214.9 84.5 all-reduce.17
where the time goes:
time: 3450 us; the launch traced here: 3440 us
  waiting for transfers between devices  2220 us (64%)
  local copies, waits for them, and re-layouts  516 us (15%)
  other arithmetic  507 us (15%)
  matrix products  174 us (5%)
    all_to_all x1, waiting for transfers between devices, shards(): lax.all_to_all(buffer, ('row', 'col'), split_axis=0, concat_axis=0, tiled...  1440 us
    psum x6, waiting for transfers between devices, broadcast(): return lax.psum(jnp.where(mine, x, jnp.zeros_like(x)), axis)  770 us
    another operation x29, other arithmetic, shards(): lower_factor = jnp.linalg.cholesky(diagonal)  158 us
    dot_general x2, matrix products, shards(): lax.dot_general(factor_factor_column.reshape(-1, B), factor_across.reshap...  125 us
    add x1, other arithmetic, shards(): summed = received[0] + received[1]  111 us
    reshape x2, local copies, waits for them, and re-layouts, shards(): summed.transpose(2, 1, 3, 4, 0, 5).reshape(local_rows, B, local_cols, B)  99.2 us
    all_to_all x1, local copies, waits for them, and re-layouts, shards(): lax.all_to_all(buffer, ('row', 'col'), split_axis=0, concat_axis=0, tiled...  83.9 us
    another operation x5, other arithmetic, shards(): jax.scipy.linalg.solve_triangular(lower_factor, column_slab.reshape(-1, B...  79.5 us
  transfers between devices with their start and end apart: 7, of which 7 were waited for; matrix products, arithmetic and copies ran while one was open for 2% of the time, Pallas kernels for 0%

commit v1 on v0

v1 whole, which is shorter than its diff:
```python
import functools

import jax
import jax.numpy as jnp
from jax import lax
from jax.experimental import pallas as pl
from jax.experimental.pallas import tpu as pltpu
from jax.sharding import PartitionSpec as P

B = 512
VMEM_LIMIT = 48 * 1024 * 1024


def inverse_maps(block_maps, count):
    blocks = jnp.arange(count, dtype=jnp.int32)
    matches = block_maps[:, None, :] == blocks[None, :, None]
    present = jnp.any(matches, axis=2)
    places = jnp.arange(block_maps.shape[1], dtype=jnp.int32)
    source = jnp.sum(jnp.where(matches, places[None, None, :], 0), axis=2)
    return (source.astype(jnp.int32), present)


def combine_kernel(blocks, chunk, source_ref, present_ref, rows_ref, a_ref, b_ref, o_ref):
    J = pl.program_id(0)
    for m in range(chunk):
        keep_a = present_ref[J] * rows_ref[m] > 0
        keep_b = present_ref[blocks + J] * rows_ref[chunk + m] > 0
        o_ref[0, m, 0] = jnp.where(keep_a, a_ref[0, :, m, 0], 0.0) + jnp.where(
            keep_b, b_ref[0, :, m, 0], 0.0
        )


def combine(received, source, present, rows_present, column_count):
    _, half_count, chunk, _, slice_rows, slice_cols = received.shape
    blocks = source.shape[1]
    local_cols = blocks // column_count

    def child_block(child):
        return pl.BlockSpec(
            (1, half_count, chunk, 1, slice_rows, slice_cols),
            lambda J, source, present, rows: (child, 0, 0, source[child * blocks + J], 0, 0),
        )

    return pl.pallas_call(
        functools.partial(combine_kernel, blocks, chunk),
        grid_spec=pltpu.PrefetchScalarGridSpec(
            num_scalar_prefetch=3,
            grid=(blocks,),
            in_specs=[child_block(0), child_block(1)],
            out_specs=pl.BlockSpec(
                (1, chunk, 1, half_count, slice_rows, slice_cols),
                lambda J, source, present, rows: (
                    lax.rem(J, column_count), 0, lax.div(J, column_count), 0, 0, 0
                ),
            ),
        ),
        out_shape=jax.ShapeDtypeStruct(
            (column_count, chunk, local_cols, half_count, slice_rows, slice_cols), jnp.float32
        ),
        compiler_params=pltpu.CompilerParams(vmem_limit_bytes=VMEM_LIMIT),
        cost_estimate=pl.CostEstimate(
            flops=received.size, bytes_accessed=12 * received.size, transcendentals=0
        ),
    )(
        source.reshape(-1),
        present.astype(jnp.int32).reshape(-1),
        rows_present.astype(jnp.int32).reshape(-1),
        received,
        received,
    )


def split(x):
    high = x.astype(jnp.bfloat16)
    low = (x - high.astype(jnp.float32)).astype(jnp.bfloat16)
    return high, low


def update_kernel(first, row_count, column_count, place_ref, *refs):
    piece_ref, diag_ref, left_ref, right_ref, o_ref = refs[-5:]
    I = place_ref[0] + row_count * (first + pl.program_id(0))
    J = place_ref[1] + column_count * pl.program_id(1)
    _, _, _, half_count, slice_rows, slice_cols = piece_ref.shape

    @pl.when((I < 2) & (J >= 2))
    def _():
        o_ref[...] = jnp.zeros_like(o_ref)

    for k in range(2):
        @pl.when(J == k)
        def _():
            o_ref[...] = left_ref[:, 0, :, k * B : (k + 1) * B].reshape(B, B)

    @pl.when((I >= 2) & (J >= 2))
    def _():
        dims = (((1,), (1,)), ((), ()))
        dot = functools.partial(
            lax.dot_general, dimension_numbers=dims, preferred_element_type=jnp.float32
        )
        left_high, left_low = split(left_ref[:, 0].reshape(B, 2 * B))
        right_high, right_low = split(right_ref[:, 0].reshape(B, 2 * B))
        product = dot(left_high, right_low) + dot(left_low, right_high)
        product = product + dot(left_high, right_high)
        for h in range(half_count):
            columns = slice(h * slice_cols, (h + 1) * slice_cols)
            part = piece_ref[:, 0, 0, h].reshape(B, slice_cols)
            o_ref[:, columns] = part - product[:, columns]

    @pl.when((I == J) & (I >= 2))
    def _():
        same = lax.broadcasted_iota(jnp.int32, (B, B), 0) == lax.broadcasted_iota(
            jnp.int32, (B, B), 1
        )
        o_ref[...] += jnp.where(same, diag_ref[0], 0.0)


def update(previous, pieces, diag_table, left, right, place, first, local_rows, row_count):
    column_count, chunk, local_cols, half_count, slice_rows, slice_cols = pieces.shape
    aliased = previous is not None
    in_specs = [
        pl.BlockSpec(
            (column_count, 1, 1, half_count, slice_rows, slice_cols),
            lambda m, n, place: (0, m, n, 0, 0, 0),
        ),
        pl.BlockSpec(
            (1, 1, B), lambda m, n, place: (place[0] + row_count * (first + m), 0, 0)
        ),
        pl.BlockSpec(
            (column_count, 1, slice_rows, 2 * B), lambda m, n, place: (0, first + m, 0, 0)
        ),
        pl.BlockSpec((column_count, 1, slice_rows, 2 * B), lambda m, n, place: (0, n, 0, 0)),
    ]
    operands = [pieces, diag_table, left, right]
    if aliased:
        in_specs = [pl.BlockSpec(memory_space=pl.ANY)] + in_specs
        operands = [previous] + operands
    size = chunk * local_cols * B * B
    return pl.pallas_call(
        functools.partial(update_kernel, first, row_count, column_count),
        grid_spec=pltpu.PrefetchScalarGridSpec(
            num_scalar_prefetch=1,
            grid=(chunk, local_cols),
            in_specs=in_specs,
            out_specs=pl.BlockSpec((B, B), lambda m, n, place: (first + m, n)),
        ),
        out_shape=jax.ShapeDtypeStruct((local_rows * B, local_cols * B), jnp.float32),
        input_output_aliases={1: 0} if aliased else {},
        compiler_params=pltpu.CompilerParams(vmem_limit_bytes=VMEM_LIMIT),
        cost_estimate=pl.CostEstimate(
            flops=size * 12 * B, bytes_accessed=16 * size, transcendentals=0
        ),
    )(place, *operands)


def shards(child_fronts, parent_diagonal, block_maps):
    row_count = lax.axis_size("row")
    column_count = lax.axis_size("col")
    row_index = lax.axis_index("row")
    column_index = lax.axis_index("col")
    half_count = row_count // 2
    blocks = parent_diagonal.shape[0] // B
    local_rows = blocks // row_count
    local_cols = blocks // column_count
    slice_rows = B // column_count
    slice_cols = 2 * B // row_count
    child_blocks = block_maps.shape[1]
    source, present = inverse_maps(block_maps, blocks)
    my_source = lax.dynamic_index_in_dim(source, row_index // half_count, 0, keepdims=False)
    row_blocks = jnp.arange(local_rows, dtype=jnp.int32) * row_count + row_index
    rows_present = jnp.take(present, row_blocks, axis=1, mode="clip")
    by_owner = my_source.reshape(local_rows, row_count).T
    diag_table = parent_diagonal.reshape(blocks, 1, B)
    place = jnp.stack([row_index, column_index]).astype(jnp.int32)

    by_block = child_fronts.transpose(0, 2, 1, 3)

    panel = jnp.take(by_block, my_source[:2], axis=1, mode="clip")
    panel = jnp.take(panel, by_owner.reshape(-1), axis=0, mode="clip")
    panel = panel.reshape(row_count, local_rows, 2, slice_rows, slice_cols)
    panel = lax.all_to_all(panel, "row", split_axis=0, concat_axis=0, tiled=True)
    panel = panel.reshape(2, half_count, local_rows, 2, slice_rows, slice_cols)
    keep = rows_present[:, :, None] & present[:, None, :2]
    panel = jnp.where(keep[:, None, :, :, None, None], panel, 0.0)
    panel = (panel[0] + panel[1]).transpose(1, 3, 2, 0, 4)
    panel = panel.reshape(local_rows, slice_rows, 2 * B)
    positions = (
        row_blocks[:, None] * B
        + column_index * slice_rows
        + jnp.arange(slice_rows, dtype=jnp.int32)[None, :]
    )
    on_diagonal = positions[:, :, None] == jnp.arange(2 * B, dtype=jnp.int32)[None, None, :]
    panel = panel + jnp.where(on_diagonal, parent_diagonal[None, None, : 2 * B], 0.0)

    corner = lax.all_gather(panel[0], ("row", "col"), axis=0, tiled=False)
    corner = corner.reshape(row_count * B, 2 * B)[: 2 * B]
    lower = lax.linalg.cholesky(corner, symmetrize_input=False)
    solved = jax.scipy.linalg.solve_triangular(
        lower, panel.reshape(-1, 2 * B).T, lower=True
    ).T.reshape(local_rows, slice_rows, 2 * B)
    own = lax.dynamic_slice_in_dim(
        lower,
        jnp.minimum(row_index, 1) * B + column_index * slice_rows,
        slice_rows,
        axis=0,
    )
    solved = jnp.where((row_blocks < 2)[:, None, None], own[None], solved)
    left = lax.all_gather(solved, "col", axis=0, tiled=False)
    owner_rows = (
        jnp.arange(local_cols, dtype=jnp.int32) * column_count + column_index
    ) // row_count
    right = jnp.take(left, owner_rows, axis=1, mode="clip")
    mine = row_index == lax.rem(column_index, row_count)
    right = lax.psum(jnp.where(mine, right, 0.0), "row")

    chunks = min(4, local_rows)
    chunk = local_rows // chunks
    pieces = []
    for q in range(chunks):
        rows = slice(q * chunk, (q + 1) * chunk)
        buffer = jnp.take(by_block, by_owner[:, rows].reshape(-1), axis=0, mode="clip")
        buffer = buffer.reshape(row_count, chunk, child_blocks, slice_rows, slice_cols)
        received = lax.all_to_all(buffer, "row", split_axis=0, concat_axis=0, tiled=True)
        received = received.reshape(
            2, half_count, chunk, child_blocks, slice_rows, slice_cols
        )
        summed = combine(received, source, present, rows_present[:, rows], column_count)
        pieces.append(
            lax.all_to_all(summed, "col", split_axis=0, concat_axis=0, tiled=True)
        )
    result = None
    for q in range(chunks):
        result = update(
            result, pieces[q], diag_table, left, right, place, q * chunk, local_rows, row_count
        )
    return result


def solution(mesh):
    return jax.shard_map(
        shards,
        mesh=mesh,
        in_specs=(P(None, "col", None, "row"), P(), P()),
        out_specs=P("row", "col"),
        check_vma=False,
    )
```

time: 3450 us -> 1680 us (0.49)
  waiting for transfers between devices: 2220 us -> 990 us
  local copies, waits for them, and re-layouts: 516 us -> 128 us
  other arithmetic: 507 us -> 276 us
  Pallas kernels: 0 us -> 162 us
  matrix products: 174 us -> 39 us
  starting transfers between devices: 7.5 us -> 52 us
    psum x6 -> x1, waiting for transfers between devices: 770 us -> 153 us  [shards(): right = lax.psum(jnp.where(mine, right, 0.0), 'row')]
    all_to_all x1 -> x9, waiting for transfers between devices: 1440 us -> 837 us  [the longest x4 408 us: shards(): lax.all_to_all(buffer, 'row', split_axis=0, concat_axis=0, tiled=True)]
    pallas_call x0 -> x8, Pallas kernels: none -> 162 us  [the longest x4 84.6 us: combine(): pl.pallas_call(functools.partial(combine_kernel, blocks, chunk), grid_spe...]
    reshape x5 -> x13, local copies, waits for them, and re-layouts: 147 us -> 11 us  [the longest x3 10.2 us: shards(): panel = panel.reshape(local_rows, slice_rows, 2 * B)]
    dot_general x2 -> x0, matrix products: 125 us -> none  [shards(): lax.dot_general(factor_factor_column.reshape(-1, B), factor_across.reshap...]
    add x3, other arithmetic: 125 us -> 1.84 us  [the longest x1 1.76 us: shards(): panel + jnp.where(on_diagonal, parent_diagonal[None, None, :2 * B], 0.0)]
    all_to_all x1 -> x0, local copies, waits for them, and re-layouts: 83.9 us -> none  [shards(): lax.all_to_all(buffer, ('row', 'col'), split_axis=0, concat_axis=0, tiled...]
    transpose x3 -> x2, other arithmetic: 81.4 us -> 1.95 us  [the longest x1 1.67 us: shards(): panel.reshape(-1, 2 * B)]
  transfers between devices with their start and end apart: 7 -> 12, of which waited for: 7 -> 8; matrix products, arithmetic and copies ran while one was open for 2% -> 25% of each run, Pallas kernels for 0% -> 9%
where the time goes in v1:
time: 1680 us; the launch traced here: 1670 us
  waiting for transfers between devices  990 us (59%)
  other arithmetic  276 us (16%)
  Pallas kernels  162 us (10%)
  local copies, waits for them, and re-layouts  128 us (8%)
  starting transfers between devices  52 us (3%)
  matrix products  39 us (2%)
  between operations  19.2 us (1%)
    all_to_all x4, waiting for transfers between devices, shards(): lax.all_to_all(buffer, 'row', split_axis=0, concat_axis=0, tiled=True)  408 us
    all_to_all x4, waiting for transfers between devices, shards(): lax.all_to_all(summed, 'col', split_axis=0, concat_axis=0, tiled=True)  394 us
    another operation x31, other arithmetic, shards(): lower = lax.linalg.cholesky(corner, symmetrize_input=False)  173 us
    psum x1, waiting for transfers between devices, shards(): right = lax.psum(jnp.where(mine, right, 0.0), 'row')  153 us
    another operation x3, other arithmetic, shards(): jax.scipy.linalg.solve_triangular(lower, panel.reshape(-1, 2 * B).T, lowe...  85.2 us
    pallas_call x4, Pallas kernels, combine(): pl.pallas_call(functools.partial(combine_kernel, blocks, chunk), grid_spe...  84.6 us
    pallas_call x4, Pallas kernels, update(): pl.pallas_call(functools.partial(update_kernel, first, row_count, column_...  77 us
    gather x4, local copies, waits for them, and re-layouts, shards(): jnp.take(by_block, by_owner[:, rows].reshape(-1), axis=0, mode='clip')  54.5 us
  transfers between devices with their start and end apart: 12, of which 8 were waited for; matrix products, arithmetic and copies ran while one was open for 25% of the time, Pallas kernels for 9%

profile of v1, /device:TPU:0, one launch (start us, length us, event | category | flops | bytes accessed | tf_op | source)
XLA Modules:
  0.0 1665.9 jit_solution(1221980587908032983)
XLA Ops:
  9.1 9.2 gather_fusion.2
  25.9 13.8 gather_fusion.1
  39.7 35.1 %all-to-all-done.2 = f32[4,8,2,64,256]{4,3,2,1,0:T(8,128)} async-done(((f32[4,8,2,64,256]{4,3,2,1,0:T(8,128)}), f32[4,8,2,64,256]{4,3,2,1,0:T(8,128)}, u32[]{:S(2)}, u32[]{:S(2)}) %all-to-all-start.2) | async-done | bytes 4194336 | tf_op jit(solution)/shard_map/all_to_all | solution.py:180
  74.8 5.9 all-to-all-start
  80.7 13.5 gather_fusion.5
  94.2 102.1 %all-to-all-done = f32[4,2,20,64,256]{4,3,2,1,0:T(8,128)} async-done(((f32[4,2,20,64,256]{4,3,2,1,0:T(8,128)}), f32[4,2,20,64,256]{4,3,2,1,0:T(8,128)}, u32[]{:S(2)}, u32[]{:S(2)}) %all-to-all-start) | async-done | bytes 10485792 | tf_op jit(solution)/shard_map/all_to_all | solution.py:222
  196.3 6.0 all-to-all-start.3
  202.7 13.8 gather_fusion.6
  216.5 101.5 %all-to-all-done.3 = f32[4,2,20,64,256]{4,3,2,1,0:T(8,128)} async-done(((f32[4,2,20,64,256]{4,3,2,1,0:T(8,128)}), f32[4,2,20,64,256]{4,3,2,1,0:T(8,128)}, u32[]{:S(2)}, u32[]{:S(2)}) %all-to-all-start.3) | async-done | bytes 10485792 | tf_op jit(solution)/shard_map/all_to_all | solution.py:222
  318.0 6.1 all-to-all-start.5
  336.9 13.5 gather_fusion.7
  350.4 109.9 %all-to-all-done.5 = f32[4,2,20,64,256]{4,3,2,1,0:T(8,128)} async-done(((f32[4,2,20,64,256]{4,3,2,1,0:T(8,128)}), f32[4,2,20,64,256]{4,3,2,1,0:T(8,128)}, u32[]{:S(2)}, u32[]{:S(2)}) %all-to-all-start.5) | async-done | bytes 10485792 | tf_op jit(solution)/shard_map/all_to_all | solution.py:222
  460.3 6.0 all-to-all-start.7
  466.7 20.9 %shard_map.37 = f32[8,2,4,2,64,256]{5,4,3,2,1,0:T(8,128)} custom-call(s32[64]{0:T(128)S(1)} %reshape.280.source_ref, s32[64]{0:T(128)S(1)} %reshape.323.present_ref, s32[4]{0:T(128)S(1)} %reshape.325.rows_ref, f32[2,2,2,20,64,256]{5,4,3,2,1,0:T(8,128)} %bitcast.7.a_ref.b_ref, f32[2,2,2,20,64,256]{5,4,3,2,1,0:T(8,128)} %bitcast.7.a_ref.b_ref), custom_call_target="tpu_custom_call" | custom-call | flops 2621440 | bytes 31457280 | tf_op jit(solution)/shard_map/pallas_call | solution.py:44
  487.7 94.3 %all-to-all-done.7 = f32[4,2,20,64,256]{4,3,2,1,0:T(8,128)} async-done(((f32[4,2,20,64,256]{4,3,2,1,0:T(8,128)}), f32[4,2,20,64,256]{4,3,2,1,0:T(8,128)}, u32[]{:S(2)}, u32[]{:S(2)}) %all-to-all-start.7) | async-done | bytes 10485792 | tf_op jit(solution)/shard_map/all_to_all | solution.py:222
  582.0 6.6 all-to-all-start.1
  596.8 21.4 %shard_map.39 = f32[8,2,4,2,64,256]{5,4,3,2,1,0:T(8,128)} custom-call(s32[64]{0:T(128)S(1)} %reshape.280.source_ref, s32[64]{0:T(128)S(1)} %reshape.323.present_ref, s32[4]{0:T(128)S(1)} %reshape.328.rows_ref, f32[2,2,2,20,64,256]{5,4,3,2,1,0:T(8,128)} %bitcast.45.a_ref.b_ref, f32[2,2,2,20,64,256]{5,4,3,2,1,0:T(8,128)} %bitcast.45.a_ref.b_ref), custom_call_target="tpu_custom_call" | custom-call | flops 2621440 | bytes 31457280 | tf_op jit(solution)/shard_map/pallas_call | solution.py:44
  622.7 11.7 cholesky.223
  636.9 9.8 custom-call.48
  650.7 11.7 cholesky.244
  663.0 9.9 custom-call.49
  676.3 11.7 cholesky.468
  688.7 9.8 custom-call.50
  702.1 11.9 cholesky.487
  714.6 9.8 custom-call.51
  727.9 11.7 cholesky.506
  740.3 9.8 custom-call.52
  753.8 11.7 cholesky.526
  766.2 9.8 custom-call.53
  779.0 11.7 cholesky.546
  791.4 10.0 custom-call.54
  804.0 11.7 cholesky.564
  826.6 6.6 fusion.1
  833.2 6.1 all-to-all-start.4
  839.4 23.3 %while.1 = (s32[]{:T(128)}, f32[1024,1024]{1,0:T(8,128)}, s32[8,2]{0,1:T(2,128)S(1)}, f32[8,128,128]{2,1,0:T(8,128)S(1)}, s32[]{:T(128)}) while((s32[]{:T(128)}, f32[1024,1024]{1,0:T(8,128)}, s32[8,2]{0,1:T(2,128)S(1)}, f32[8,128,128]{2,1,0:T(8,128)S(1)}, s32[]{:T(128)}) %tuple.67), condition=%wide.while_cond, body=%wide.while_body.sunk | while | flops 2 | bytes 131181 | solution.py:197
  862.7 78.6 %custom-call.55 = f32[8,128,128]{1,2,0:T(8,128)S(1)} custom-call(f32[8,128,128]{2,1,0:T(8,128)S(1)} %get-tuple-element.12), custom_call_target="InvertDiagBlocksLowerTriangular" | custom-call | tf_op jit(solution)/shard_map/jit(_solve_triangular)/triangular_solve | solution.py:197
  962.9 21.3 %shard_map.41 = f32[8,2,4,2,64,256]{5,4,3,2,1,0:T(8,128)} custom-call(s32[64]{0:T(128)S(1)} %reshape.280.source_ref, s32[64]{0:T(128)S(1)} %reshape.323.present_ref, s32[4]{0:T(128)S(1)} %reshape.330.rows_ref, f32[2,2,2,20,64,256]{5,4,3,2,1,0:T(8,128)} %bitcast.47.a_ref.b_ref, f32[2,2,2,20,64,256]{5,4,3,2,1,0:T(8,128)} %bitcast.47.a_ref.b_ref), custom_call_target="tpu_custom_call" | custom-call | flops 2621440 | bytes 31457280 | tf_op jit(solution)/shard_map/pallas_call | solution.py:44
  984.3 122.2 %all-to-all-done.4.refs_1_ = f32[8,2,4,2,64,256]{5,4,3,2,1,0:T(8,128)} async-done(((f32[8,2,4,2,64,256]{5,4,3,2,1,0:T(8,128)}), f32[8,2,4,2,64,256]{5,4,3,2,1,0:T(8,128)}, u32[]{:S(2)}, u32[]{:S(2)}) %all-to-all-start.4) | async-done | bytes 8388640 | tf_op jit(solution)/shard_map/all_to_all | solution.py:228
  1106.5 5.0 all-to-all-start.6
  1111.6 21.0 %shard_map.43 = f32[8,2,4,2,64,256]{5,4,3,2,1,0:T(8,128)} custom-call(s32[64]{0:T(128)S(1)} %reshape.280.source_ref, s32[64]{0:T(128)S(1)} %reshape.323.present_ref, s32[4]{0:T(128)S(1)} %reshape.332.rows_ref, f32[2,2,2,20,64,256]{5,4,3,2,1,0:T(8,128)} %bitcast.49.a_ref.b_ref, f32[2,2,2,20,64,256]{5,4,3,2,1,0:T(8,128)} %bitcast.49.a_ref.b_ref), custom_call_target="tpu_custom_call" | custom-call | flops 2621440 | bytes 31457280 | tf_op jit(solution)/shard_map/pallas_call | solution.py:44
  1132.6 271.7 %all-to-all-done.6.refs_1_ = f32[8,2,4,2,64,256]{5,4,3,2,1,0:T(8,128)} async-done(((f32[8,2,4,2,64,256]{5,4,3,2,1,0:T(8,128)}), f32[8,2,4,2,64,256]{5,4,3,2,1,0:T(8,128)}, u32[]{:S(2)}, u32[]{:S(2)}) %all-to-all-start.6) | async-done | bytes 8388640 | tf_op jit(solution)/shard_map/all_to_all | solution.py:228
  1409.7 10.3 gather_fusion.4
  1419.9 8.5 fusion
  1428.5 153.4 %all-reduce.3.cloned.1.call-done.refs_3_.refs_4_ = f32[8,4,64,1024]{3,2,1,0:T(8,128)} async-done(((f32[8,4,64,1024]{3,2,1,0:T(8,128)}), f32[8,4,64,1024]{3,2,1,0:T(8,128)}) %all-reduce.3.cloned.1.call-update) | async-done | bytes 8388624 | tf_op jit(solution)/shard_map/psum | solution.py:213
  1581.9 17.4 %shard_map.38.refs_0_ = f32[4096,2048]{1,0:T(8,128)} custom-call(s32[2]{0:T(128)S(1)} %pad_add_fusion.place_ref, f32[8,2,4,2,64,256]{5,4,3,2,1,0:T(8,128)} %all-to-all-done.1.refs_0_, f32[32,1,512]{2,1,0:T(1,128)S(1)} %bitcast.136, f32[8,8,64,1024]{3,2,1,0:T(8,128)} %all-gather.5.cloned.1.call-done.refs_2_.refs_3_, ...), custom_call_target="tpu_custom_call" | custom-call | flops 12884901888 | bytes 33554432 | tf_op jit(solution)/shard_map/pallas_call | solution.py:138
  1599.3 19.9 %shard_map.40.refs_0_ = f32[4096,2048]{1,0:T(8,128)} custom-call(s32[2]{0:T(128)S(1)} %pad_add_fusion.place_ref, f32[4096,2048]{1,0:T(8,128)} %shard_map.38.refs_0_, f32[8,2,4,2,64,256]{5,4,3,2,1,0:T(8,128)} %all-to-all-done.4.refs_1_, f32[32,1,512]{2,1,0:T(1,128)S(1)} %bitcast.137, ...), custom_call_target="tpu_custom_call", output_to_operand_aliasing={{}: (1, {})} | custom-call | flops 12884901888 | bytes 33554432 | tf_op jit(solution)/shard_map/pallas_call | solution.py:138
  1619.2 19.9 %shard_map.42.refs_0_ = f32[4096,2048]{1,0:T(8,128)} custom-call(s32[2]{0:T(128)S(1)} %pad_add_fusion.place_ref, f32[4096,2048]{1,0:T(8,128)} %shard_map.40.refs_0_, f32[8,2,4,2,64,256]{5,4,3,2,1,0:T(8,128)} %all-to-all-done.6.refs_1_, f32[32,1,512]{2,1,0:T(1,128)S(1)} %bitcast.138, ...), custom_call_target="tpu_custom_call", output_to_operand_aliasing={{}: (1, {})} | custom-call | flops 12884901888 | bytes 33554432 | tf_op jit(solution)/shard_map/pallas_call | solution.py:138
  1639.0 19.9 %shard_map.44 = f32[4096,2048]{1,0:T(8,128)} custom-call(s32[2]{0:T(128)S(1)} %pad_add_fusion.place_ref, f32[4096,2048]{1,0:T(8,128)} %shard_map.42.refs_0_, f32[8,2,4,2,64,256]{5,4,3,2,1,0:T(8,128)} %all-to-all-done.8.refs_1_, f32[32,1,512]{2,1,0:T(1,128)S(1)} %bitcast.139, ...), custom_call_target="tpu_custom_call", output_to_operand_aliasing={{}: (1, {})} | custom-call | flops 12884901888 | bytes 33554432 | tf_op jit(solution)/shard_map/pallas_call | solution.py:138
  (167 shorter events, 122.2 us)
Async XLA Ops:
  21.1 53.7 %all-to-all-start.2 = ((f32[4,8,2,64,256]{4,3,2,1,0:T(8,128)}), f32[4,8,2,64,256]{4,3,2,1,0:T(8,128)}, u32[]{:S(2)}, u32[]{:S(2)}) async-start(f32[4,8,2,64,256]{4,3,2,1,0:T(8,128)} %bitcast.150), calls=%async_computation.2 | async-start | bytes 8388608 | tf_op jit(solution)/shard_map/all_to_all | solution.py:180
  74.8 121.6 %all-to-all-start = ((f32[4,2,20,64,256]{4,3,2,1,0:T(8,128)}), f32[4,2,20,64,256]{4,3,2,1,0:T(8,128)}, u32[]{:S(2)}, u32[]{:S(2)}) async-start(f32[4,2,20,64,256]{4,3,2,1,0:T(8,128)} %bitcast.148), calls=%async_computation | async-start | bytes 20971520 | tf_op jit(solution)/shard_map/all_to_all | solution.py:222
  196.3 121.6 %all-to-all-start.3 = ((f32[4,2,20,64,256]{4,3,2,1,0:T(8,128)}), f32[4,2,20,64,256]{4,3,2,1,0:T(8,128)}, u32[]{:S(2)}, u32[]{:S(2)}) async-start(f32[4,2,20,64,256]{4,3,2,1,0:T(8,128)} %bitcast.147), calls=%async_computation.3 | async-start | bytes 20971520 | tf_op jit(solution)/shard_map/all_to_all | solution.py:222
  318.0 6.2 copy-start.6
  318.0 7.2 copy-start
  318.0 142.3 %all-to-all-start.5 = ((f32[4,2,20,64,256]{4,3,2,1,0:T(8,128)}), f32[4,2,20,64,256]{4,3,2,1,0:T(8,128)}, u32[]{:S(2)}, u32[]{:S(2)}) async-start(f32[4,2,20,64,256]{4,3,2,1,0:T(8,128)} %bitcast.145), calls=%async_computation.5 | async-start | bytes 20971520 | tf_op jit(solution)/shard_map/all_to_all | solution.py:222
  324.1 294.1 %all-gather.3.cloned.1.call-start = ((), (), s32[]{:S(2)}) async-start(), calls=%async_computation.9 | async-start | bytes 8650752 | tf_op jit(solution)/shard_map/all_gather | solution.py:194
  325.1 2.8 copy-start.4
  328.3 6.9 slice-start
  460.3 121.7 %all-to-all-start.7 = ((f32[4,2,20,64,256]{4,3,2,1,0:T(8,128)}), f32[4,2,20,64,256]{4,3,2,1,0:T(8,128)}, u32[]{:S(2)}, u32[]{:S(2)}) async-start(f32[4,2,20,64,256]{4,3,2,1,0:T(8,128)} %bitcast.146), calls=%async_computation.7 | async-start | bytes 20971520 | tf_op jit(solution)/shard_map/all_to_all | solution.py:222
  487.7 101.0 %copy-start.5 = (s32[8,64]{1,0:T(8,128)S(1)}, s32[8,64]{1,0:T(8,128)}, u32[]{:S(2)}) copy-start(s32[8,64]{1,0:T(8,128)} %copy-done.4) | copy-start | bytes 6148
  582.0 251.2 %all-to-all-start.1 = ((f32[8,2,4,2,64,256]{5,4,3,2,1,0:T(8,128)}), f32[8,2,4,2,64,256]{5,4,3,2,1,0:T(8,128)}, u32[]{:S(2)}, u32[]{:S(2)}) async-start(f32[8,2,4,2,64,256]{5,4,3,2,1,0:T(8,128)} %shard_map.37), calls=%async_computation.1 | async-start | bytes 16777216 | tf_op jit(solution)/shard_map/all_to_all | solution.py:228
  620.8 1.9 copy-start.1
  833.2 108.1 %copy-start.2 = (f32[1024,512]{1,0:T(8,128)S(1)}, f32[1024,512]{1,0:T(8,128)}, u32[]{:S(2)}) copy-start(f32[1024,512]{1,0:T(8,128)} %add_bitcast_fusion) | copy-start | bytes 6291460
  833.2 273.3 %all-to-all-start.4 = ((f32[8,2,4,2,64,256]{5,4,3,2,1,0:T(8,128)}), f32[8,2,4,2,64,256]{5,4,3,2,1,0:T(8,128)}, u32[]{:S(2)}, u32[]{:S(2)}) async-start(f32[8,2,4,2,64,256]{5,4,3,2,1,0:T(8,128)} %shard_map.39), calls=%async_computation.4 | async-start | bytes 16777216 | tf_op jit(solution)/shard_map/all_to_all | solution.py:228
  839.3 570.3 %all-gather.5.cloned.1.call-start = ((), (), s32[]{:S(2)}) async-start(), calls=%async_computation.10 | async-start | bytes 18874368 | tf_op jit(solution)/shard_map/all_gather | solution.py:207
  956.8 1.3 copy-start.3
  1106.5 297.9 %all-to-all-start.6 = ((f32[8,2,4,2,64,256]{5,4,3,2,1,0:T(8,128)}), f32[8,2,4,2,64,256]{5,4,3,2,1,0:T(8,128)}, u32[]{:S(2)}, u32[]{:S(2)}) async-start(f32[8,2,4,2,64,256]{5,4,3,2,1,0:T(8,128)} %shard_map.41), calls=%async_computation.6 | async-start | bytes 16777216 | tf_op jit(solution)/shard_map/all_to_all | solution.py:228
  1404.3 234.7 %all-to-all-start.8 = ((f32[8,2,4,2,64,256]{5,4,3,2,1,0:T(8,128)}), f32[8,2,4,2,64,256]{5,4,3,2,1,0:T(8,128)}, u32[]{:S(2)}, u32[]{:S(2)}) async-start(f32[8,2,4,2,64,256]{5,4,3,2,1,0:T(8,128)} %shard_map.43), calls=%async_computation.8 | async-start | bytes 16777216 | tf_op jit(solution)/shard_map/all_to_all | solution.py:228
  1409.3 172.6 %all-reduce.3.cloned.1.call-start = ((), (), s32[]{:S(2)}) async-start(), calls=%async_computation.11 | async-start | bytes 16777216 | tf_op jit(solution)/shard_map/psum | solution.py:213
Sparse Core Ops, SparseCore 0:
  337.0 98.4 all-gather.2
  962.9 410.2 all-gather.4
  1428.6 153.3 all-reduce.2
